TPU v7x, 32 devices: a whole 2x2x4 slice. The times are simulated.
32 devices in a mesh: dp: 8 (over z, core), ctx: 4 (over y, x).
Axes of the slice: x: 2, y: 2, z: 4, core: 2. Of those that a mesh axis runs over, the one named last changes fastest.
Arguments:
- activations: bfloat16 [8, 512, 2048], P('dp', 'ctx'), may hold values from -8 to 8
- out_grads: bfloat16 [8, 512, 2048], P('dp', 'ctx'), may hold values from -64 to 64
- segment_ids: int32 [8, 512], P('dp', 'ctx'), may hold values from -1 to 1, as said below
Outputs:
- weight_grad: float32 [2048, 2048], P('ctx', 'dp')
- clip_factors: float32 [8, 2], P('dp')
Inputs may be any that keep to these rules, and one draw needn't show every extreme that they name: `segment_ids`: each sequence holds 2 documents, numbered in order; each occupies one or more whole consecutive blocks of 128 tokens, and -1 (padding) occurs only at the end of a document's last block; every document has at least one token.
All inputs are finite; a program needn't handle non-finite values.
Results may differ from a plain program's by a relative error of at most 0.0016.
Values may be sent and summed in bfloat16 or wider, within the bound.
A program may use at most 128 MiB of HBM per device.

v0:
```python
import jax
import jax.numpy as jnp
from jax import lax
from jax.sharding import PartitionSpec as P

BLOCK = 128


clip_bound = 600.0


def body(activations, out_grads, segment_ids):
    own_acts = activations[0]
    own_grads = out_grads[0]
    own_ids = segment_ids[0]
    groups = lax.axis_size("ctx")
    my_slot = lax.axis_index("ctx")
    row_count = own_acts.shape[1] // groups
    all_ids = lax.all_gather(own_ids, "ctx", axis=0, tiled=True)
    seq_len = all_ids.shape[0]
    doc_count = seq_len // BLOCK // 2
    doc_range = jnp.arange(doc_count, dtype=jnp.int32)
    own_hot = (own_ids[:, None] == doc_range[None, :]).astype(jnp.float32)
    row_begin = my_slot * row_count
    piece_acts = lax.all_gather(own_acts, "ctx", axis=0, tiled=True)
    piece_grads = lax.all_gather(own_grads, "ctx", axis=0, tiled=True)
    piece_rows = piece_acts.shape[0]
    gram_in = lax.dot_general(
        own_acts, piece_acts, (((1,), (1,)), ((), ())), preferred_element_type=jnp.float32
    )
    gram_out = lax.dot_general(
        own_grads, piece_grads, (((1,), (1,)), ((), ())), preferred_element_type=jnp.float32
    )
    same_doc = (own_ids[:, None] == all_ids[None, :]) & (own_ids[:, None] >= 0)
    products = (
        jnp.where(same_doc, gram_in * gram_out, jnp.float32(0.0))
        * jnp.ones((piece_rows,), jnp.float32)[None, :]
    )
    per_token = jnp.sum(products, axis=1)
    added = jnp.dot(per_token, own_hot, precision=lax.Precision.HIGHEST)
    own_rows = lax.dynamic_slice_in_dim(piece_acts, row_begin, row_count, 1)
    rows_store = own_rows
    grad_store = piece_grads
    partial_norms, rows_store, grad_store = (added, rows_store, grad_store)
    norm_sq = lax.psum(partial_norms, "ctx")
    clip_factor = clip_bound / jnp.sqrt(jnp.maximum(norm_sq, clip_bound * clip_bound))
    all_hot = (all_ids[:, None] == doc_range[None, :]).astype(jnp.float32)
    token_clip = jnp.dot(all_hot, clip_factor, precision=lax.Precision.HIGHEST)
    scaled = (grad_store.astype(jnp.float32) * token_clip[:, None]).astype(jnp.bfloat16)
    partial_grad = lax.dot_general(
        rows_store, scaled, (((0,), (0,)), ((), ())), preferred_element_type=jnp.float32
    )
    weight_grad = lax.psum_scatter(partial_grad, "dp", scatter_dimension=1, tiled=True)
    return (weight_grad, clip_factor[None, :])


def solution(mesh):
    placed = (P("dp", "ctx", None), P("dp", "ctx", None), P("dp", "ctx"))
    return jax.shard_map(
        body, mesh=mesh, in_specs=placed, out_specs=(P("ctx", "dp"), P("dp", None)), check_vma=False
    )
```

profile of v0, /device:TPU:0, one launch (start us, length us, event | category | flops | bytes accessed | tf_op | source)
XLA Modules:
  0.0 158.3 jit_solution(13028730980319273208)
XLA Ops:
  7.2 0.0 copy-start.1
  7.2 0.0 copy-start.2
  7.2 0.0 all-gather.6.cloned.1.call-start
  7.2 0.7 all-gather.6.cloned.1.call-update
  7.9 0.0 all-gather.8.cloned.1.call-start
  8.0 0.7 all-gather.8.cloned.1.call-update
  8.7 0.0 reduce-scatter.2.cloned.1.call-start
  8.7 9.5 %all-gather.2 = s32[1,512]{1,0:T(1,128)S(1)} all-gather(s32[1,128]{1,0:T(1,128)} %param.5), channel_id=4, replica_groups=mesh['dp'=8,'ctx'=4] {'ctx'}, dimensions={1}, use_global_device_ids=true | all-gather | bytes 2560 | tf_op jit(solution)/shard_map/all_gather | solution.py:19
  18.2 0.7 broadcast_compare_fusion
  18.9 29.1 %all-gather.6.cloned.1.call-done = bf16[1,512,2048]{2,1,0:T(8,128)(2,1)} async-done(((bf16[1,128,2048]{2,1,0:T(8,128)(2,1)}), bf16[1,512,2048]{2,1,0:T(8,128)(2,1)}) %all-gather.6.cloned.1.call-update) | async-done | bytes 2097168 | tf_op jit(solution)/shard_map/all_gather | solution.py:25
  47.9 2.6 %fusion.1 = f32[128,512]{1,0:T(8,128)S(1)} fusion(bf16[1,512,2048]{2,1,0:T(8,128)(2,1)} %all-gather.6.cloned.1.call-done, bf16[1,128,2048]{2,1,0:T(8,128)(2,1)} %param.3), kind=kOutput, calls=%fused_computation.2 | convolution fusion | flops 268435456 | bytes 2883584 | tf_op jit(solution)/shard_map/dot_general | solution.py:28
  50.5 34.6 %all-gather.8.cloned.1.call-done = bf16[1,512,2048]{2,1,0:T(8,128)(2,1)} async-done(((bf16[1,128,2048]{2,1,0:T(8,128)(2,1)}), bf16[1,512,2048]{2,1,0:T(8,128)(2,1)}) %all-gather.8.cloned.1.call-update) | async-done | bytes 2097168 | tf_op jit(solution)/shard_map/all_gather | solution.py:26
  85.1 0.0 copy-start
  85.1 0.0 copy-done.1
  85.1 0.0 copy-done.2
  85.1 2.7 %fusion.13 = f32[128]{0:T(128)S(1)} fusion(f32[128,512]{1,0:T(8,128)S(1)} %fusion.1, bf16[1,512,2048]{2,1,0:T(8,128)(2,1)} %all-gather.8.cloned.1.call-done, bf16[1,128,2048]{2,1,0:T(8,128)(2,1)S(1)} %copy-done.1, s32[512]{0:T(512)S(1)} %bitcast.39, s32[128]{0:T(128)S(1)} %bitcast.42, pred[128]{0:T(512)(128)(4,1)S(1)} %broadcast_compare_fusion), kind=kOutput, calls=%fused_computation.10 | convolution fusion | flops 268763008 | bytes 2886784 | tf_op jit(solution)/shard_map/dot_general | solution.py:31
  87.8 0.2 convolution_bitcast_fusion
  88.0 8.9 %psum.7 = f32[2]{0:T(128)S(1)} all-reduce(f32[2]{0:T(128)S(1)} %convolution_bitcast_fusion), channel_id=1, replica_groups=mesh['dp'=8,'ctx'=4] {'ctx'}, use_global_device_ids=true, to_apply=%region_1.2 | all-reduce | flops 2 | bytes 16 | tf_op jit(solution)/shard_map/psum | solution.py:45
  96.9 0.3 fusion.20
  97.2 0.0 copy-done
  97.2 4.4 %fusion = f32[512,2048]{1,0:T(8,128)} fusion(bf16[1,512,2048]{2,1,0:T(8,128)(2,1)S(1)} %copy-done, f32[512]{0:T(512)S(1)} %bitcast.41, bf16[1,512,2048]{2,1,0:T(8,128)(2,1)} %all-gather.6.cloned.1.call-done, s32[]{:T(128)S(6)} %select_n.7), kind=kOutput, calls=%fused_computation.1 | convolution fusion | flops 1076887552 | bytes 6817796 | tf_op jit(solution)/shard_map/dot_general | solution.py:50
  101.6 0.0 reduce-scatter.2.cloned.1.call-update
  101.6 0.5 fusion.26
  102.1 49.6 %reduce-scatter.2.cloned.1.call-done = f32[512,256]{1,0:T(8,128)} async-done(((f32[512,2048]{1,0:T(8,128)}), f32[512,256]{1,0:T(8,128)}) %reduce-scatter.2.cloned.1.call-update) | async-done | bytes 524304 | tf_op jit(solution)/shard_map/reduce_scatter | solution.py:53
Async XLA Ops:
  7.2 77.9 %copy-start.1 = (bf16[1,128,2048]{2,1,0:T(8,128)(2,1)S(1)}, bf16[1,128,2048]{2,1,0:T(8,128)(2,1)}, u32[]{:S(2)}) copy-start(bf16[1,128,2048]{2,1,0:T(8,128)(2,1)} %param.4) | copy-start | bytes 1572868
  7.2 77.9 %copy-start.2 = (s32[1,128]{1,0:T(1,128)S(1)}, s32[1,128]{1,0:T(1,128)}, u32[]{:S(2)}) copy-start(s32[1,128]{1,0:T(1,128)} %param.5) | copy-start | bytes 1540
  7.2 40.7 %all-gather.6.cloned.1.call-start = ((), (), s32[]{:S(2)}) async-start(), calls=%async_computation.2 | async-start | bytes 2621440 | tf_op jit(solution)/shard_map/all_gather | solution.py:25
  7.9 77.2 %all-gather.8.cloned.1.call-start = ((), (), s32[]{:S(2)}) async-start(), calls=%async_computation.3 | async-start | bytes 2621440 | tf_op jit(solution)/shard_map/all_gather | solution.py:26
  8.7 143.1 %reduce-scatter.2.cloned.1.call-start = ((), (), s32[]{:S(2)}) async-start(), calls=%async_computation.1 | async-start | bytes 4718592 | tf_op jit(solution)/shard_map/reduce_scatter | solution.py:53
  85.1 12.1 %copy-start = (bf16[1,512,2048]{2,1,0:T(8,128)(2,1)S(1)}, bf16[1,512,2048]{2,1,0:T(8,128)(2,1)}, u32[]{:S(2)}) copy-start(bf16[1,512,2048]{2,1,0:T(8,128)(2,1)} %all-gather.8.cloned.1.call-done) | copy-start | bytes 6291460
Sparse Core Ops, SparseCore 0:
  9.9 38.0 all-gather.5
  49.8 35.2 all-gather.7
  101.7 49.9 reduce-scatter.1
where the time goes:
time: 159 us; the launch traced here: 158 us
  waiting for transfers between devices  115 us (72%)
  blocking collectives  18.4 us (12%)
  between operations  13.8 us (9%)
  matrix products  10.1 us (6%)
    reduce_scatter x1, waiting for transfers between devices, body(): lax.psum_scatter(partial_grad, 'dp', scatter_dimension=1, tiled=True)  49.6 us
    all_gather x1, waiting for transfers between devices, body(): piece_grads = lax.all_gather(own_grads, 'ctx', axis=0, tiled=True)  34.6 us
    all_gather x1, waiting for transfers between devices, body(): piece_acts = lax.all_gather(own_acts, 'ctx', axis=0, tiled=True)  29.1 us
    all_gather x1, blocking collectives, body(): all_ids = lax.all_gather(own_ids, 'ctx', axis=0, tiled=True)  9.47 us
    psum x1, blocking collectives, body(): norm_sq = lax.psum(partial_norms, 'ctx')  8.93 us
    dot_general x1, matrix products, body(): lax.dot_general(rows_store, scaled, (((0,), (0,)), ((), ())), preferred_e...  4.37 us
  transfers between devices with their start and end apart: 3, of which 3 were waited for; matrix products, arithmetic and copies ran while one was open for 2% of the time, Pallas kernels for 0%

commit v1 on v0

v1 whole, which is shorter than its diff:
```python
import functools

import jax
import jax.numpy as jnp
from jax import lax
from jax.experimental import pallas as pl
from jax.experimental.pallas import tpu as pltpu
from jax.sharding import PartitionSpec as P

BLOCK = 128
LANES = 128
GROUP = 4

clip_bound = 600.0


def plain_body(activations, out_grads, segment_ids):
    own_acts = activations[0]
    own_grads = out_grads[0]
    own_ids = segment_ids[0]
    groups = lax.axis_size("ctx")
    my_slot = lax.axis_index("ctx")
    row_count = own_acts.shape[1] // groups
    all_ids = lax.all_gather(own_ids, "ctx", axis=0, tiled=True)
    doc_count = all_ids.shape[0] // BLOCK // 2
    doc_range = jnp.arange(doc_count, dtype=jnp.int32)
    own_hot = (own_ids[:, None] == doc_range[None, :]).astype(jnp.float32)
    all_acts = lax.all_gather(own_acts, "ctx", axis=0, tiled=True)
    all_grads = lax.all_gather(own_grads, "ctx", axis=0, tiled=True)
    gram_in = lax.dot_general(
        own_acts, all_acts, (((1,), (1,)), ((), ())), preferred_element_type=jnp.float32
    )
    gram_out = lax.dot_general(
        own_grads, all_grads, (((1,), (1,)), ((), ())), preferred_element_type=jnp.float32
    )
    same_doc = (own_ids[:, None] == all_ids[None, :]) & (own_ids[:, None] >= 0)
    per_token = jnp.sum(jnp.where(same_doc, gram_in * gram_out, jnp.float32(0.0)), axis=1)
    norm_sq = lax.psum(jnp.dot(per_token, own_hot, precision=lax.Precision.HIGHEST), "ctx")
    clip_factor = clip_bound / jnp.sqrt(jnp.maximum(norm_sq, clip_bound * clip_bound))
    own_rows = lax.dynamic_slice_in_dim(all_acts, my_slot * row_count, row_count, 1)
    all_hot = (all_ids[:, None] == doc_range[None, :]).astype(jnp.float32)
    token_clip = jnp.dot(all_hot, clip_factor, precision=lax.Precision.HIGHEST)
    scaled = (all_grads.astype(jnp.float32) * token_clip[:, None]).astype(jnp.bfloat16)
    partial_grad = lax.dot_general(
        own_rows, scaled, (((0,), (0,)), ((), ())), preferred_element_type=jnp.float32
    )
    weight_grad = lax.psum_scatter(partial_grad, "dp", scatter_dimension=1, tiled=True)
    return (weight_grad, clip_factor[None, :])


def kernel(docs, his, n, a_ref, g_ref, id_ref, out_ref, clip_ref,
           acts, grads, staged, ids, shares, scaled, outgoing, incoming,
           sa_plane, sa_z, sa_sib, sa_fwd, ra, sg_split, sg_a, sg_b, sg_fwd, rg,
           s_id, r_id, s_norm, r_norm, s_out, r_out):
    R = GROUP
    dp = lax.axis_index("dp")
    c = lax.axis_index("ctx")
    hi = dp // R
    r = lax.rem(dp, R)
    base = hi * R
    rows = acts.shape[3]
    width = out_ref.shape[1]

    def flip(v, bits):
        out = v
        for bit in (1, 2):
            if bits & bit:
                has = lax.rem(out // bit, 2)
                out = out + bit * (1 - 2 * has)
        return out

    rx = [flip(r, b) for b in range(R)]
    cx = [flip(c, b) for b in range(n)]
    peers = [(rb, cb) for rb in range(R) for cb in range(n) if rb or cb]

    barrier = pltpu.get_barrier_semaphore()
    for rb, cb in peers:
        pl.semaphore_signal(barrier, inc=1, device_id=(base + rx[rb], cx[cb]),
                            device_id_type=pl.DeviceIdType.MESH)
    others = []
    for h in range(1, his):
        there = lax.rem(hi + h, his)
        others.append(there * R + r)
        pl.semaphore_signal(barrier, inc=1, device_id=(others[-1], c),
                            device_id_type=pl.DeviceIdType.MESH)

    tok = id_ref[...]
    keep = jnp.transpose(jnp.broadcast_to((tok >= 0).astype(jnp.float32), (BLOCK, BLOCK)))
    keep = jnp.concatenate([keep] * (width // LANES), axis=1) > 0.5
    for q in range(R):
        for p in range(his):
            block = lax.rem(hi + 1 + p, his) * R + q
            piece = g_ref[:, pl.ds(pl.multiple_of(block * width, LANES), width)]
            staged[q, :, p * width:(p + 1) * width] = jnp.where(
                keep, piece.astype(jnp.float32), 0.0).astype(jnp.bfloat16)
    ids[r, c] = tok
    grads[r, c] = staged[r]
    acts[r, c] = a_ref[:, pl.ds(pl.multiple_of(c * rows, LANES), rows)]

    pl.semaphore_wait(barrier, len(peers) + his - 1)

    started = []

    def send(src, dst, ssem, rsem, to):
        cp = pltpu.make_async_remote_copy(src_ref=src, dst_ref=dst, send_sem=ssem, recv_sem=rsem,
                                          device_id=to, device_id_type=pl.DeviceIdType.MESH)
        cp.start()
        started.append(cp)

    def arrive(dst, rsem):
        pltpu.make_async_copy(dst, dst, rsem).wait()

    for b in (2, 3, 1):
        send(staged.at[rx[b]], grads.at[r, c], sg_split.at[b], rg.at[r, c], (base + rx[b], c))
    for b in (1, 2, 3):
        cols = pl.ds(pl.multiple_of(cx[b] * rows, LANES), rows)
        send(a_ref.at[:, cols], acts.at[r, c], sa_plane.at[b], ra.at[r, c], (dp, cx[b]))
    for k, (rb, cb) in enumerate(peers):
        send(ids.at[r, c], ids.at[r, c], s_id.at[k], r_id.at[rb, cb], (base + rx[rb], cx[cb]))

    def pass_acts(cb):
        slot = acts.at[r, cx[cb]]
        send(slot, slot, sa_z.at[cb], ra.at[r, cx[cb]], (base + rx[2], c))
        send(slot, slot, sa_sib.at[cb], ra.at[r, cx[cb]], (base + rx[1], c))

    def gather_grads(rb):
        slot = grads.at[rx[rb], c]
        send(slot, slot, sg_a.at[rb], rg.at[rx[rb], c], (dp, cx[1]))
        send(slot, slot, sg_b.at[rb], rg.at[rx[rb], c], (dp, cx[2]))

    def forward_grads(rb):
        came, to = (1, 2) if rb in (0, 2) else (2, 1)
        slot = grads.at[rx[rb], cx[came]]
        arrive(slot, rg.at[rx[rb], cx[came]])
        send(slot, slot, sg_fwd.at[rb], rg.at[rx[rb], cx[came]], (dp, cx[to]))

    def forward_acts(cb):
        slot = acts.at[rx[2], cx[cb]]
        arrive(slot, ra.at[rx[2], cx[cb]])
        send(slot, slot, sa_fwd.at[cb], ra.at[rx[2], cx[cb]], (base + rx[1], c))

    gather_grads(0)
    pass_acts(0)
    for b in (1, 2, 3):
        arrive(grads.at[rx[b], c], rg.at[rx[b], c])
        gather_grads(b)
        arrive(acts.at[r, cx[b]], ra.at[r, cx[b]])
        pass_acts(b)
    for b in (0, 1, 2, 3):
        forward_acts(b)
        forward_grads(b)

    for rb, cb in peers:
        arrive(ids.at[rx[rb], cx[cb]], r_id.at[rb, cb])
    for cb in range(n):
        for rb in (1, 3):
            arrive(acts.at[rx[rb], cx[cb]], ra.at[rx[rb], cx[cb]])
    for rb in range(R):
        for cb in ((2, 3) if rb in (0, 2) else (1, 3)):
            arrive(grads.at[rx[rb], cx[cb]], rg.at[rx[rb], cx[cb]])

    seq = n * BLOCK
    wide = acts.shape[3]
    cols = grads.shape[3]
    table = shares.shape[2:]
    row_at = lax.broadcasted_iota(jnp.int32, table, 0)
    nt = (((1,), (1,)), ((), ()))

    def doc_rows(s):
        return [jnp.broadcast_to(jnp.max(ids[s, i], axis=1, keepdims=True), (1, BLOCK))
                for i in range(n)]

    def norm_step(s, total):
        A = acts[s].reshape(seq, wide)
        G = grads[s].reshape(seq, cols)
        prod = (lax.dot_general(A, A, nt, preferred_element_type=jnp.float32)
                * lax.dot_general(G, G, nt, preferred_element_type=jnp.float32))
        dr = doc_rows(s)
        along = jnp.concatenate(dr, axis=1)
        v = jnp.zeros((1, seq), jnp.float32)
        for i in range(n):
            u = jnp.sum(prod[i * BLOCK:(i + 1) * BLOCK], axis=0, keepdims=True)
            mine = jnp.concatenate([dr[i]] * n, axis=1)
            v = v + jnp.where(along == mine, u, 0.0)
        for b in range(docs):
            nb = jnp.sum(jnp.where(along == b, v, 0.0), axis=1, keepdims=True)
            total = jnp.where(row_at == s * docs + b, jnp.broadcast_to(nb, table), total)
        return total

    total = lax.fori_loop(0, R, norm_step, jnp.zeros(table, jnp.float32))
    shares[r, c] = total
    for k, (rb, cb) in enumerate(peers):
        send(shares.at[r, c], shares.at[r, c], s_norm.at[k], r_norm.at[rb, cb],
             (base + rx[rb], cx[cb]))
    for rb, cb in peers:
        arrive(shares.at[rx[rb], cx[cb]], r_norm.at[rb, cb])
    norm = jnp.zeros(table, jnp.float32)
    for i in range(R):
        for j in range(n):
            norm = norm + shares[i, j]
    clip = clip_bound / jnp.sqrt(jnp.maximum(norm, clip_bound * clip_bound))

    lane_at = lax.broadcasted_iota(jnp.int32, (1, LANES), 1)
    own = jnp.zeros((1, LANES), jnp.float32)
    for b in range(docs):
        picked = jnp.sum(jnp.where(row_at == r * docs + b, clip, 0.0), axis=0, keepdims=True)
        own = jnp.where(lane_at == b, picked, own)
    clip_ref[...] = own[:, :docs]

    for s in range(R):
        dr = doc_rows(s)
        for i in range(n):
            factor = jnp.zeros((1, LANES), jnp.float32)
            for b in range(docs):
                factor = jnp.where(dr[i] == b, clip[s * docs + b:s * docs + b + 1], factor)
            factor = jnp.concatenate([factor] * (cols // LANES), axis=1)
            at = (s * n + i) * BLOCK
            scaled[at:at + BLOCK] = (grads[s, i].astype(jnp.float32) * factor).astype(jnp.bfloat16)

    tn = (((0,), (0,)), ((), ()))
    whole = acts[...].reshape(R * seq, wide)
    for p in range(his):
        part = lax.dot_general(whole, scaled[:, p * width:(p + 1) * width], tn,
                               preferred_element_type=jnp.float32)
        if p < his - 1:
            outgoing[p] = part.astype(jnp.bfloat16)
            send(outgoing.at[p], incoming.at[p], s_out.at[p], r_out.at[p], (others[p], c))
        else:
            out_ref[...] = part
    for p in range(his - 1):
        arrive(incoming.at[p], r_out.at[p])
        out_ref[...] += incoming[p].astype(jnp.float32)
    for cp in started:
        cp.wait_send()


def group_body(activations, out_grads, segment_ids):
    n = lax.axis_size("ctx")
    size = lax.axis_size("dp")
    his = size // GROUP
    tokens, d_in = activations.shape[1:]
    d_out = out_grads.shape[2]
    rows, width = d_in // n, d_out // size
    docs = n * tokens // BLOCK // 2
    table = -(-GROUP * docs // 8) * 8
    bf, f32 = jnp.bfloat16, jnp.float32
    dma = pltpu.SemaphoreType.DMA
    vm = pl.BlockSpec(memory_space=pltpu.VMEM)
    peers = GROUP * n - 1
    return pl.pallas_call(
        functools.partial(kernel, docs, his, n),
        out_shape=(jax.ShapeDtypeStruct((rows, width), f32), jax.ShapeDtypeStruct((1, docs), f32)),
        in_specs=[vm, vm, vm],
        out_specs=(vm, vm),
        scratch_shapes=[
            pltpu.VMEM((GROUP, n, tokens, rows), bf),
            pltpu.VMEM((GROUP, n, tokens, his * width), bf),
            pltpu.VMEM((GROUP, tokens, his * width), bf),
            pltpu.VMEM((GROUP, n, 1, tokens), jnp.int32),
            pltpu.VMEM((GROUP, n, table, LANES), f32),
            pltpu.VMEM((GROUP * n * tokens, his * width), bf),
            pltpu.VMEM((his - 1, rows, width), bf),
            pltpu.VMEM((his - 1, rows, width), bf),
            dma((n,)), dma((n,)), dma((n,)), dma((n,)), dma((GROUP, n)),
            dma((GROUP,)), dma((GROUP,)), dma((GROUP,)), dma((GROUP,)), dma((GROUP, n)),
            dma((peers,)), dma((GROUP, n)), dma((peers,)), dma((GROUP, n)),
            dma((his - 1,)), dma((his - 1,)),
        ],
        compiler_params=pltpu.CompilerParams(
            collective_id=0, has_side_effects=True, vmem_limit_bytes=48 * 1024 * 1024),
    )(activations[0], out_grads[0], segment_ids)


def body(activations, out_grads, segment_ids):
    n = lax.axis_size("ctx")
    size = lax.axis_size("dp")
    rows, width = activations.shape[2] // n, out_grads.shape[2] // size
    fits = (n == GROUP and size % GROUP == 0 and size > GROUP and activations.shape[1] == BLOCK
            and rows % LANES == 0 and width % LANES == 0)
    chosen = group_body if fits else plain_body
    return chosen(activations, out_grads, segment_ids)


def solution(mesh):
    placed = (P("dp", "ctx", None), P("dp", "ctx", None), P("dp", "ctx"))
    return jax.shard_map(
        body, mesh=mesh, in_specs=placed, out_specs=(P("ctx", "dp"), P("dp", None)), check_vma=False
    )
```

time: 159 us -> 58.3 us (0.37)
  waiting for transfers between devices: 115 us -> 0 us
  Pallas kernels: 0 us -> 53.4 us
  blocking collectives: 18.4 us -> 0 us
  between operations: 13.8 us -> 0.65 us
  matrix products: 10.1 us -> 0 us
  local copies, waits for them, and re-layouts: 0.01 us -> 4.04 us
    all_gather x2 -> x0, waiting for transfers between devices: 63.6 us -> none  [the longest x1 34.6 us: body(): piece_grads = lax.all_gather(own_grads, 'ctx', axis=0, tiled=True)]
    pallas_call x0 -> x1, Pallas kernels: none -> 53.4 us  [group_body(): pl.pallas_call(functools.partial(kernel, docs, his, n), out_shape=(jax.Sh...]
    reduce_scatter x1 -> x0, waiting for transfers between devices: 49.6 us -> none  [body(): lax.psum_scatter(partial_grad, 'dp', scatter_dimension=1, tiled=True)]
    dot_general x5 -> x0, matrix products: 10.1 us -> none  [the longest x1 4.37 us: body(): lax.dot_general(rows_store, scaled, (((0,), (0,)), ((), ())), preferred_e...]
    all_gather x1 -> x0, blocking collectives: 9.47 us -> none  [body(): all_ids = lax.all_gather(own_ids, 'ctx', axis=0, tiled=True)]
    psum x1 -> x0, blocking collectives: 8.93 us -> none  [body(): norm_sq = lax.psum(partial_norms, 'ctx')]
    unnamed x6 -> x8, local copies, waits for them, and re-layouts: 0.01 us -> 4.04 us
  transfers between devices with their start and end apart: 3 -> 0, of which waited for: 3 -> 0; matrix products, arithmetic and copies ran while one was open for 2% -> 0% of each run, Pallas kernels for 0% -> 0%
where the time goes in v1:
time: 58.3 us; the launch traced here: 58.1 us
  Pallas kernels  53.4 us (92%)
  local copies, waits for them, and re-layouts  4.04 us (7%)
  between operations  0.65 us (1%)
    pallas_call x1, Pallas kernels, group_body(): pl.pallas_call(functools.partial(kernel, docs, his, n), out_shape=(jax.Sh...  53.4 us
    unnamed x8, local copies, waits for them, and re-layouts  4.04 us

profile of v1, /device:TPU:0, one launch (start us, length us, event | category | flops | bytes accessed | tf_op | source)
XLA Modules:
  0.0 58.1 jit_solution(11492012665337848337)
XLA Ops:
  0.6 0.0 copy-start.2
  0.6 0.6 %copy-done.2 = s32[1,128]{1,0:T(1,128)S(1)} copy-done((s32[1,128]{1,0:T(1,128)S(1)}, s32[1,128]{1,0:T(1,128)}, u32[]{:S(2)}) %copy-start.2) | copy-done | bytes 536
  1.3 0.0 copy-start
  1.3 1.0 %copy-done = bf16[1,128,2048]{2,1,0:T(8,128)(2,1)S(1)} copy-done((bf16[1,128,2048]{2,1,0:T(8,128)(2,1)S(1)}, bf16[1,128,2048]{2,1,0:T(8,128)(2,1)}, u32[]{:S(2)}) %copy-start) | copy-done | bytes 524312
  2.3 0.0 copy-start.1
  2.3 1.0 %copy-done.1 = bf16[1,128,2048]{2,1,0:T(8,128)(2,1)S(1)} copy-done((bf16[1,128,2048]{2,1,0:T(8,128)(2,1)S(1)}, bf16[1,128,2048]{2,1,0:T(8,128)(2,1)}, u32[]{:S(2)}) %copy-start.1) | copy-done | bytes 524312
  3.4 53.4 %shard_map.50 = (f32[512,256]{1,0:T(8,128)S(1)}, f32[1,2]{1,0:T(1,128)S(1)}) custom-call(bf16[128,2048]{1,0:T(8,128)(2,1)S(1)} %bitcast.2, bf16[128,2048]{1,0:T(8,128)(2,1)S(1)} %bitcast.3, s32[1,128]{1,0:T(1,128)S(1)} %copy-done.2), custom_call_target="tpu_custom_call" | custom-call | tf_op jit(solution)/shard_map/pallas_call | solution.py:250
  56.8 0.8 %copy.7 = f32[512,256]{1,0:T(8,128)} copy(f32[512,256]{1,0:T(8,128)S(1)} %get-tuple-element.4) | data formatting | bytes 1048576
  57.6 0.5 copy.8
Async XLA Ops:
  0.6 0.7 %copy-start.2 = (s32[1,128]{1,0:T(1,128)S(1)}, s32[1,128]{1,0:T(1,128)}, u32[]{:S(2)}) copy-start(s32[1,128]{1,0:T(1,128)} %id_ref.1) | copy-start | bytes 1540
  1.3 1.0 %copy-start = (bf16[1,128,2048]{2,1,0:T(8,128)(2,1)S(1)}, bf16[1,128,2048]{2,1,0:T(8,128)(2,1)}, u32[]{:S(2)}) copy-start(bf16[1,128,2048]{2,1,0:T(8,128)(2,1)} %param.3) | copy-start | bytes 1572868
  2.3 1.0 %copy-start.1 = (bf16[1,128,2048]{2,1,0:T(8,128)(2,1)S(1)}, bf16[1,128,2048]{2,1,0:T(8,128)(2,1)}, u32[]{:S(2)}) copy-start(bf16[1,128,2048]{2,1,0:T(8,128)(2,1)} %param.4) | copy-start | bytes 1572868

commit v2 on v1

--- a/solution.py
+++ b/solution.py
@@ -49,7 +49,7 @@
 
 
 def kernel(docs, his, n, a_ref, g_ref, id_ref, out_ref, clip_ref,
-           acts, grads, staged, ids, shares, scaled, outgoing, incoming,
+           acts, grads, raw, staged, ids, shares, turned, gram_in, scaled, outgoing, incoming, s_own,
            sa_plane, sa_z, sa_sib, sa_fwd, ra, sg_split, sg_a, sg_b, sg_fwd, rg,
            s_id, r_id, s_norm, r_norm, s_out, r_out):
     R = GROUP
@@ -73,6 +73,14 @@
     cx = [flip(c, b) for b in range(n)]
     peers = [(rb, cb) for rb in range(R) for cb in range(n) if rb or cb]
 
+    local = [
+        pltpu.make_async_copy(id_ref, ids.at[r, c], s_own.at[0]),
+        pltpu.make_async_copy(g_ref.at[0], raw, s_own.at[1]),
+        pltpu.make_async_copy(
+            a_ref.at[0, :, pl.ds(pl.multiple_of(c * rows, LANES), rows)], acts.at[r, c], s_own.at[2]),
+    ]
+    for cp in local:
+        cp.start()
     barrier = pltpu.get_barrier_semaphore()
     for rb, cb in peers:
         pl.semaphore_signal(barrier, inc=1, device_id=(base + rx[rb], cx[cb]),
@@ -80,22 +88,24 @@
     others = []
     for h in range(1, his):
         there = lax.rem(hi + h, his)
-        others.append(there * R + r)
+        others.append(there * R + rx[2])
         pl.semaphore_signal(barrier, inc=1, device_id=(others[-1], c),
                             device_id_type=pl.DeviceIdType.MESH)
 
-    tok = id_ref[...]
+    local[0].wait()
+    tok = ids[r, c]
     keep = jnp.transpose(jnp.broadcast_to((tok >= 0).astype(jnp.float32), (BLOCK, BLOCK)))
     keep = jnp.concatenate([keep] * (width // LANES), axis=1) > 0.5
+    local[1].wait()
     for q in range(R):
         for p in range(his):
-            block = lax.rem(hi + 1 + p, his) * R + q
-            piece = g_ref[:, pl.ds(pl.multiple_of(block * width, LANES), width)]
+            there = lax.rem(hi + 1 + p, his)
+            block = there * R + (q if p == his - 1 else q ^ 2)
+            piece = raw[:, pl.ds(pl.multiple_of(block * width, LANES), width)]
             staged[q, :, p * width:(p + 1) * width] = jnp.where(
                 keep, piece.astype(jnp.float32), 0.0).astype(jnp.bfloat16)
-    ids[r, c] = tok
     grads[r, c] = staged[r]
-    acts[r, c] = a_ref[:, pl.ds(pl.multiple_of(c * rows, LANES), rows)]
+    local[2].wait()
 
     pl.semaphore_wait(barrier, len(peers) + his - 1)
 
@@ -114,7 +124,7 @@
         send(staged.at[rx[b]], grads.at[r, c], sg_split.at[b], rg.at[r, c], (base + rx[b], c))
     for b in (1, 2, 3):
         cols = pl.ds(pl.multiple_of(cx[b] * rows, LANES), rows)
-        send(a_ref.at[:, cols], acts.at[r, c], sa_plane.at[b], ra.at[r, c], (dp, cx[b]))
+        send(a_ref.at[0, :, cols], acts.at[r, c], sa_plane.at[b], ra.at[r, c], (dp, cx[b]))
     for k, (rb, cb) in enumerate(peers):
         send(ids.at[r, c], ids.at[r, c], s_id.at[k], r_id.at[rb, cb], (base + rx[rb], cx[cb]))
 
@@ -146,22 +156,10 @@
         gather_grads(b)
         arrive(acts.at[r, cx[b]], ra.at[r, cx[b]])
         pass_acts(b)
-    for b in (0, 1, 2, 3):
-        forward_acts(b)
-        forward_grads(b)
-
-    for rb, cb in peers:
-        arrive(ids.at[rx[rb], cx[cb]], r_id.at[rb, cb])
-    for cb in range(n):
-        for rb in (1, 3):
-            arrive(acts.at[rx[rb], cx[cb]], ra.at[rx[rb], cx[cb]])
-    for rb in range(R):
-        for cb in ((2, 3) if rb in (0, 2) else (1, 3)):
-            arrive(grads.at[rx[rb], cx[cb]], rg.at[rx[rb], cx[cb]])
-
     seq = n * BLOCK
     wide = acts.shape[3]
     cols = grads.shape[3]
+    pieces, step = outgoing.shape[1:3]
     table = shares.shape[2:]
     row_at = lax.broadcasted_iota(jnp.int32, table, 0)
     nt = (((1,), (1,)), ((), ()))
@@ -170,24 +168,46 @@
         return [jnp.broadcast_to(jnp.max(ids[s, i], axis=1, keepdims=True), (1, BLOCK))
                 for i in range(n)]
 
-    def norm_step(s, total):
+    def prepare(rb):
+        s = rx[rb]
+        for i in range(n):
+            at = pl.multiple_of((s * n + i) * BLOCK, LANES)
+            turned[:, pl.ds(at, BLOCK)] = jnp.transpose(acts[s, i])
         A = acts[s].reshape(seq, wide)
-        G = grads[s].reshape(seq, cols)
-        prod = (lax.dot_general(A, A, nt, preferred_element_type=jnp.float32)
-                * lax.dot_general(G, G, nt, preferred_element_type=jnp.float32))
+        gram = lax.dot_general(A, A, nt, preferred_element_type=jnp.float32)
         dr = doc_rows(s)
         along = jnp.concatenate(dr, axis=1)
-        v = jnp.zeros((1, seq), jnp.float32)
         for i in range(n):
-            u = jnp.sum(prod[i * BLOCK:(i + 1) * BLOCK], axis=0, keepdims=True)
             mine = jnp.concatenate([dr[i]] * n, axis=1)
-            v = v + jnp.where(along == mine, u, 0.0)
+            at = slice(i * BLOCK, (i + 1) * BLOCK)
+            gram_in[rb, at] = jnp.where(along == mine, gram[at], 0.0)
+
+    def norm_step(rb, total):
+        s = rx[rb]
+        for cb in ((2, 3) if rb in (0, 2) else (1, 3)):
+            arrive(grads.at[s, cx[cb]], rg.at[s, cx[cb]])
+        G = grads[s].reshape(seq, cols)
+        gram_out = lax.dot_general(G, G, nt, preferred_element_type=jnp.float32)
+        v = jnp.sum(gram_in[rb] * gram_out, axis=0, keepdims=True)
+        along = jnp.concatenate(doc_rows(s), axis=1)
         for b in range(docs):
             nb = jnp.sum(jnp.where(along == b, v, 0.0), axis=1, keepdims=True)
             total = jnp.where(row_at == s * docs + b, jnp.broadcast_to(nb, table), total)
         return total
 
-    total = lax.fori_loop(0, R, norm_step, jnp.zeros(table, jnp.float32))
+    for b in range(n):
+        forward_acts(b)
+    for rb, cb in peers:
+        arrive(ids.at[rx[rb], cx[cb]], r_id.at[rb, cb])
+    for rb in (0, 2, 1, 3):
+        if rb in (1, 3):
+            for cb in range(n):
+                arrive(acts.at[rx[rb], cx[cb]], ra.at[rx[rb], cx[cb]])
+        forward_grads({0: 0, 2: 1, 1: 2, 3: 3}[rb])
+        prepare(rb)
+    total = jnp.zeros(table, jnp.float32)
+    for rb in range(R):
+        total = norm_step(rb, total)
     shares[r, c] = total
     for k, (rb, cb) in enumerate(peers):
         send(shares.at[r, c], shares.at[r, c], s_norm.at[k], r_norm.at[rb, cb],
@@ -207,29 +227,36 @@
         own = jnp.where(lane_at == b, picked, own)
     clip_ref[...] = own[:, :docs]
 
+    factors = []
     for s in range(R):
         dr = doc_rows(s)
         for i in range(n):
             factor = jnp.zeros((1, LANES), jnp.float32)
             for b in range(docs):
                 factor = jnp.where(dr[i] == b, clip[s * docs + b:s * docs + b + 1], factor)
-            factor = jnp.concatenate([factor] * (cols // LANES), axis=1)
-            at = (s * n + i) * BLOCK
-            scaled[at:at + BLOCK] = (grads[s, i].astype(jnp.float32) * factor).astype(jnp.bfloat16)
-
-    tn = (((0,), (0,)), ((), ()))
-    whole = acts[...].reshape(R * seq, wide)
-    for p in range(his):
-        part = lax.dot_general(whole, scaled[:, p * width:(p + 1) * width], tn,
-                               preferred_element_type=jnp.float32)
-        if p < his - 1:
-            outgoing[p] = part.astype(jnp.bfloat16)
-            send(outgoing.at[p], incoming.at[p], s_out.at[p], r_out.at[p], (others[p], c))
-        else:
-            out_ref[...] = part
+            factors.append(jnp.concatenate([factor] * (width // LANES), axis=1))
+
+    def scale(p):
+        at_cols = slice(p * width, (p + 1) * width)
+        for k, factor in enumerate(factors):
+            piece = grads[k // n, k % n, :, at_cols].astype(jnp.float32) * factor
+            scaled[k * BLOCK:(k + 1) * BLOCK, at_cols] = piece.astype(jnp.bfloat16)
+
     for p in range(his - 1):
-        arrive(incoming.at[p], r_out.at[p])
-        out_ref[...] += incoming[p].astype(jnp.float32)
+        scale(p)
+        for k in range(pieces):
+            at = slice(k * step, (k + 1) * step)
+            outgoing[p, k] = jnp.dot(turned[at], scaled[:, p * width:(p + 1) * width],
+                                     preferred_element_type=jnp.float32).astype(jnp.bfloat16)
+            send(outgoing.at[p, k], incoming.at[p, k], s_out.at[p, k], r_out.at[p, k],
+                 (others[p], c))
+    scale(his - 1)
+    out_ref[...] = jnp.dot(turned[...], scaled[:, (his - 1) * width:],
+                           preferred_element_type=jnp.float32)
+    for p in range(his - 1):
+        for k in range(pieces):
+            arrive(incoming.at[p, k], r_out.at[p, k])
+            out_ref[k * step:(k + 1) * step] += incoming[p, k].astype(jnp.float32)
     for cp in started:
         cp.wait_send()
 
@@ -246,29 +273,35 @@
     bf, f32 = jnp.bfloat16, jnp.float32
     dma = pltpu.SemaphoreType.DMA
     vm = pl.BlockSpec(memory_space=pltpu.VMEM)
+    hbm = pl.BlockSpec(memory_space=pltpu.HBM)
+    pieces = rows // LANES
     peers = GROUP * n - 1
     return pl.pallas_call(
         functools.partial(kernel, docs, his, n),
         out_shape=(jax.ShapeDtypeStruct((rows, width), f32), jax.ShapeDtypeStruct((1, docs), f32)),
-        in_specs=[vm, vm, vm],
+        in_specs=[hbm, hbm, hbm],
         out_specs=(vm, vm),
         scratch_shapes=[
             pltpu.VMEM((GROUP, n, tokens, rows), bf),
             pltpu.VMEM((GROUP, n, tokens, his * width), bf),
+            pltpu.VMEM((tokens, his * GROUP * width), bf),
             pltpu.VMEM((GROUP, tokens, his * width), bf),
             pltpu.VMEM((GROUP, n, 1, tokens), jnp.int32),
             pltpu.VMEM((GROUP, n, table, LANES), f32),
+            pltpu.VMEM((rows, GROUP * n * tokens), bf),
+            pltpu.VMEM((GROUP, n * tokens, n * tokens), f32),
             pltpu.VMEM((GROUP * n * tokens, his * width), bf),
-            pltpu.VMEM((his - 1, rows, width), bf),
-            pltpu.VMEM((his - 1, rows, width), bf),
+            pltpu.VMEM((his - 1, pieces, rows // pieces, width), bf),
+            pltpu.VMEM((his - 1, pieces, rows // pieces, width), bf),
+            dma((3,)),
             dma((n,)), dma((n,)), dma((n,)), dma((n,)), dma((GROUP, n)),
             dma((GROUP,)), dma((GROUP,)), dma((GROUP,)), dma((GROUP,)), dma((GROUP, n)),
             dma((peers,)), dma((GROUP, n)), dma((peers,)), dma((GROUP, n)),
-            dma((his - 1,)), dma((his - 1,)),
+            dma((his - 1, pieces)), dma((his - 1, pieces)),
         ],
         compiler_params=pltpu.CompilerParams(
-            collective_id=0, has_side_effects=True, vmem_limit_bytes=48 * 1024 * 1024),
-    )(activations[0], out_grads[0], segment_ids)
+            collective_id=0, has_side_effects=True, vmem_limit_bytes=53 * 1024 * 1024),
+    )(activations, out_grads, segment_ids)
 
 
 def body(activations, out_grads, segment_ids):

time: 58.3 us -> 52.7 us (0.904)
  the two profiles are of different devices: /device:TPU:0 before, /device:TPU:13 now
where the time goes in v2:
time: 52.7 us; the launch traced here: 52.5 us
  Pallas kernels  49.9 us (95%)
  local copies, waits for them, and re-layouts  1.95 us (4%)
  between operations  0.65 us (1%)
    pallas_call x1, Pallas kernels, group_body(): pl.pallas_call(functools.partial(kernel, docs, his, n), out_shape=(jax.Sh...  49.9 us
    unnamed x4, local copies, waits for them, and re-layouts  1.95 us

profile of v2, /device:TPU:13, one launch (start us, length us, event | category | flops | bytes accessed | tf_op | source)
XLA Modules:
  0.0 52.5 jit_solution(17097935650410359039)
XLA Ops:
  0.6 0.0 copy-start
  0.6 0.6 %copy-done = s32[1,128]{1,0:T(1,128)S(1)} copy-done((s32[1,128]{1,0:T(1,128)S(1)}, s32[1,128]{1,0:T(1,128)}, u32[]{:S(2)}) %copy-start) | copy-done | bytes 536
  1.3 49.9 %shard_map.50 = (f32[512,256]{1,0:T(8,128)S(1)}, f32[1,2]{1,0:T(1,128)S(1)}) custom-call(bf16[1,128,2048]{2,1,0:T(8,128)(2,1)} %a_ref.1, bf16[1,128,2048]{2,1,0:T(8,128)(2,1)} %g_ref.1, s32[1,128]{1,0:T(1,128)S(1)} %copy-done), custom_call_target="tpu_custom_call" | custom-call | tf_op jit(solution)/shard_map/pallas_call | solution.py:279
  51.2 0.8 %copy.7 = f32[512,256]{1,0:T(8,128)} copy(f32[512,256]{1,0:T(8,128)S(1)} %get-tuple-element.4) | data formatting | bytes 1048576
  52.0 0.5 copy.8
Async XLA Ops:
  0.6 0.7 %copy-start = (s32[1,128]{1,0:T(1,128)S(1)}, s32[1,128]{1,0:T(1,128)}, u32[]{:S(2)}) copy-start(s32[1,128]{1,0:T(1,128)} %id_ref.1) | copy-start | bytes 1540

commit v3 on v2

--- a/solution.py
+++ b/solution.py
@@ -71,7 +71,7 @@
 
     rx = [flip(r, b) for b in range(R)]
     cx = [flip(c, b) for b in range(n)]
-    peers = [(rb, cb) for rb in range(R) for cb in range(n) if rb or cb]
+    peers = [(rb, cb) for rb in (2, 3, 0, 1) for cb in (3, 2, 1, 0) if rb or cb]
 
     local = [
         pltpu.make_async_copy(id_ref, ids.at[r, c], s_own.at[0]),

time: 52.7 us -> 52.6 us (level)
  the two profiles are of different devices: /device:TPU:13 before, /device:TPU:9 now
where the time goes in v3:
time: 52.6 us; the launch traced here: 52.5 us
  Pallas kernels  49.9 us (95%)
  local copies, waits for them, and re-layouts  1.95 us (4%)
  between operations  0.65 us (1%)
    pallas_call x1, Pallas kernels, group_body(): pl.pallas_call(functools.partial(kernel, docs, his, n), out_shape=(jax.Sh...  49.9 us
    unnamed x4, local copies, waits for them, and re-layouts  1.95 us

profile of v3, /device:TPU:9, one launch (start us, length us, event | category | flops | bytes accessed | tf_op | source)
XLA Modules:
  0.0 52.5 jit_solution(16489631999594529028)
XLA Ops:
  0.6 0.0 copy-start
  0.6 0.6 %copy-done = s32[1,128]{1,0:T(1,128)S(1)} copy-done((s32[1,128]{1,0:T(1,128)S(1)}, s32[1,128]{1,0:T(1,128)}, u32[]{:S(2)}) %copy-start) | copy-done | bytes 536
  1.3 49.9 %shard_map.50 = (f32[512,256]{1,0:T(8,128)S(1)}, f32[1,2]{1,0:T(1,128)S(1)}) custom-call(bf16[1,128,2048]{2,1,0:T(8,128)(2,1)} %a_ref.1, bf16[1,128,2048]{2,1,0:T(8,128)(2,1)} %g_ref.1, s32[1,128]{1,0:T(1,128)S(1)} %copy-done), custom_call_target="tpu_custom_call" | custom-call | tf_op jit(solution)/shard_map/pallas_call | solution.py:279
  51.2 0.8 %copy.7 = f32[512,256]{1,0:T(8,128)} copy(f32[512,256]{1,0:T(8,128)S(1)} %get-tuple-element.4) | data formatting | bytes 1048576
  52.0 0.5 copy.8
Async XLA Ops:
  0.6 0.7 %copy-start = (s32[1,128]{1,0:T(1,128)S(1)}, s32[1,128]{1,0:T(1,128)}, u32[]{:S(2)}) copy-start(s32[1,128]{1,0:T(1,128)} %id_ref.1) | copy-start | bytes 1540
